TPU v7x, 32 devices: a whole 2x2x4 slice. The times are simulated.
32 devices in a mesh: chan: 8 (over z, y), win: 4 (over x, core).
Axes of the slice: x: 2, y: 2, z: 4, core: 2. Of those that a mesh axis runs over, the one named last changes fastest.
Arguments:
- strain: float32 [64, 32, 7500], P('chan', 'win'), may hold values from -800 to 800
- sources: int32 [4, 8], replicated, may hold values from 0 to 63, as said below
Outputs:
- stacks: float32 [32, 64, 513], P('win', 'chan')
Inputs may be any that keep to these rules, and one draw needn't show every extreme that they name: `sources`: counting channels in aligned blocks of 8, the 8 channels of one round lie in different blocks, and over all rounds every block holds exactly 4 of them.
All inputs are finite; a program needn't handle non-finite values.
Results may differ from a plain program's by a relative error of at most 0.0024.
Values may be sent and summed in bfloat16 or wider, within the bound.
A program may use at most 128 MiB of HBM per device.

v0:
```python
import functools
import math

import jax
import jax.numpy as jnp
from jax import lax
from jax.experimental import pallas as pl
from jax.experimental.pallas import tpu as pltpu
from jax.sharding import PartitionSpec as P

MAX_LAG = 256
BLOCK = 128


def whiten(strain):
    mean_square = jnp.mean(strain * strain, axis=-1, keepdims=True)
    return (strain * lax.rsqrt(mean_square + 1e-06)).astype(jnp.bfloat16)


def ring_position(index, size):
    odd = lax.rem(index, 2)
    half = index // 2
    return (1 - odd) * half + odd * (size - 1 - half)


def ring_index(position, size):
    back = position // (size // 2)
    return (1 - back) * 2 * position + back * (2 * (size - 1 - position) + 1)


def kernel(
    sizes, streamed, factor, pieces_ref, local_ref, order_ref, out_ref,
    recv_ref, wide_ref, held_ref, own_ref, probe_ref, partial_ref, send_ref, land_ref,
    send_sem, recv_sem, stack_send_sem, stack_recv_sem,
):
    chan_size, win_size, lag_blocks, windows, front = sizes
    channels = recv_ref.shape[0]
    ways, _, count, depth, _ = held_ref.shape
    per_shard = ways * count
    here = ring_position(lax.axis_index("chan"), chan_size)
    win = lax.axis_index("win")
    right = ring_index(lax.rem(here + 1, chan_size), chan_size)
    left = ring_index(lax.rem(here + chan_size - 1, chan_size), chan_size)
    targets = [right, left]

    barrier = pltpu.get_barrier_semaphore()
    for chan in targets:
        pl.semaphore_signal(barrier, inc=1, device_id={"chan": chan}, device_id_type=pl.DeviceIdType.MESH)
    for step in range(1, win_size):
        peer = lax.rem(win + step, win_size)
        pl.semaphore_signal(barrier, inc=1, device_id={"win": peer}, device_id_type=pl.DeviceIdType.MESH)
    for way in range(ways):
        for item in range(count):
            held_ref[way, 0, item] = pieces_ref[local_ref[way * count + item]]
    own_ref[...] = jnp.zeros_like(own_ref)
    probe_ref[...] = jnp.zeros_like(probe_ref)
    pl.semaphore_wait(barrier, len(targets) + win_size - 1)

    row = lax.broadcasted_iota(jnp.int32, (BLOCK, BLOCK), 0)
    lane = lax.broadcasted_iota(jnp.int32, (BLOCK, BLOCK), 1)
    later = row + lane >= BLOCK - 1
    diagonal = row + lane == BLOCK - 1

    def hop(way, step, item):
        return pltpu.make_async_remote_copy(
            src_ref=held_ref.at[way, step, item],
            dst_ref=held_ref.at[way, step + 1, item],
            send_sem=send_sem.at[way, step, item],
            recv_sem=recv_sem.at[way, step, item],
            device_id={"chan": targets[way]},
            device_id_type=pl.DeviceIdType.MESH,
        )

    def stack_hop(dest, origin):
        slot = lax.rem(dest - win + win_size, win_size) - 1
        return pltpu.make_async_remote_copy(
            src_ref=partial_ref.at[origin * per_shard + dest],
            dst_ref=land_ref.at[slot, origin],
            send_sem=stack_send_sem.at[dest, origin],
            recv_sem=stack_recv_sem.at[slot, origin],
            device_id={"win": jnp.int32(dest)},
            device_id_type=pl.DeviceIdType.MESH,
        )

    def origin_of(way, step):
        position = here - step if way == 0 else here + step
        return ring_index(lax.rem(position + chan_size, chan_size), chan_size)

    def load(probe, item, step):
        for way in range(ways):
            probe[item, :depth, way * BLOCK : (way + 1) * BLOCK] = held_ref[way, step, item]

    def work(probe, item, step, channel):
        products = jnp.dot(recv_ref[channel], probe[item], preferred_element_type=jnp.float32)
        for way in range(ways):
            columns = products[:, way * BLOCK : (way + 1) * BLOCK]
            parts = [columns[k * BLOCK : (k + 1) * BLOCK] for k in range(lag_blocks + 1)]
            totals = []
            for k in range(lag_blocks):
                mixed = jnp.where(later, parts[k], parts[k + 1])
                sheared = pltpu.roll(mixed, 0, 1, stride=1, stride_axis=0)
                total = jnp.sum(sheared, axis=0, keepdims=True)
                totals.append(pltpu.roll(total, 1, 1) * factor)
            last = jnp.where(diagonal, parts[lag_blocks], 0.0)
            last = jnp.sum(jnp.sum(last, axis=0, keepdims=True), axis=1, keepdims=True)
            totals.append(jnp.broadcast_to(last * factor, (1, BLOCK)))
            place = origin_of(way, step) * per_shard + way * count + item
            partial_ref[place, pl.ds(channel, 1), :] = jnp.concatenate(totals, axis=1)

    def send_stacks(item, step):
        if not streamed:
            return
        for way in range(ways):
            dest = way * count + item

            @pl.when(win != dest)
            def _():
                stack_hop(dest, origin_of(way, step)).start()

    for way in range(ways):
        for item in range(count):
            hop(way, 0, item).start()

    reverse = jnp.where(diagonal, 1.0, 0.0).astype(jnp.bfloat16)
    inner = recv_ref.shape[2]
    reach = wide_ref.shape[1]
    wide_ref[...] = jnp.zeros_like(wide_ref)
    for channel in range(channels):
        wide_ref[channel % 2, front : front + depth, :] = pieces_ref[channel]
        flipped = lax.dot_general(
            reverse, wide_ref[channel % 2], (((1,), (1,)), ((), ())), preferred_element_type=jnp.float32
        )
        for k in range(lag_blocks + 1):
            shift = (lag_blocks - k) * windows
            moved = pltpu.roll(flipped, reach - shift, 1) if shift else flipped
            recv_ref[channel, k * BLOCK : (k + 1) * BLOCK, :] = moved[:, :inner].astype(jnp.bfloat16)

    spread = chan_size - 1 if chan_size - 1 <= channels else 0
    for item in range(count):
        load(own_ref, item, 0)
        for channel in range(channels - spread):
            work(own_ref, item, 0, channel)

    def body(step, carry):
        for item in range(count):
            for way in range(ways):
                hop(way, step - 1, item).wait_recv()

                @pl.when(step < chan_size - 1)
                def _():
                    hop(way, step, item).start()

            load(probe_ref, item, step)
            if spread:
                work(own_ref, item, 0, channels - spread + step - 1)
            for channel in range(channels):
                work(probe_ref, item, step, channel)
            send_stacks(item, step)
        return carry

    lax.fori_loop(1, chan_size, body, 0)
    for item in range(count):
        send_stacks(item, 0)
    for step in range(chan_size - 1):
        for way in range(ways):
            for item in range(count):
                hop(way, step, item).wait_send()

    per_win = out_ref.shape[0]
    if streamed:
        def arrived(index, carry):
            for slot in range(win_size - 1):
                peer = lax.rem(win + slot + 1, win_size)
                pltpu.make_async_remote_copy(
                    src_ref=partial_ref.at[index],
                    dst_ref=land_ref.at[slot, index],
                    send_sem=stack_send_sem.at[slot, index],
                    recv_sem=stack_recv_sem.at[slot, index],
                    device_id={"win": peer},
                    device_id_type=pl.DeviceIdType.MESH,
                ).wait_recv()
            return carry

        lax.fori_loop(0, chan_size, arrived, 0)
        for item in range(per_win):
            place = order_ref[win * per_win + item]
            owner = lax.div(place, per_shard)
            total = partial_ref[place]
            for slot in range(win_size - 1):
                total = total + land_ref[slot, owner]
            out_ref[item] = total[:, : out_ref.shape[2]]

        def sent(index, carry):
            for dest in range(win_size):
                @pl.when(win != dest)
                def _():
                    stack_hop(dest, index).wait_send()
            return carry

        lax.fori_loop(0, chan_size, sent, 0)
        return

    for dest in range(win_size):
        for item in range(per_win):
            send_ref[dest, item] = partial_ref[order_ref[dest * per_win + item]]

    def stack_copy(step):
        peer = lax.rem(win + step, win_size)
        return pltpu.make_async_remote_copy(
            src_ref=send_ref.at[peer],
            dst_ref=land_ref.at[step - 1],
            send_sem=stack_send_sem.at[step - 1],
            recv_sem=stack_recv_sem.at[step - 1],
            device_id={"win": peer},
            device_id_type=pl.DeviceIdType.MESH,
        )

    for step in range(1, win_size):
        stack_copy(step).start()
    for step in range(1, win_size):
        stack_copy(step).wait_recv()
    total = send_ref[win]
    for step in range(1, win_size):
        total = total + land_ref[step - 1]
    out_ref[...] = total[:, :, : out_ref.shape[2]]
    for step in range(1, win_size):
        stack_copy(step).wait_send()


def correlate(pieces, local_channel, order, windows, rounds, factor):
    channels, depth, _ = pieces.shape
    per_shard = local_channel.shape[0]
    total = order.shape[0]
    chan_size, win_size = lax.axis_size("chan"), lax.axis_size("win")
    lag_blocks = 2 * MAX_LAG // BLOCK
    lag_count = 2 * MAX_LAG + 1
    front = (lag_blocks - MAX_LAG // BLOCK) * windows
    inner = -(-depth // 256) * 256
    reach = -(-(inner + lag_blocks * windows) // BLOCK) * BLOCK
    lanes = (lag_blocks + 1) * BLOCK
    per_win = total // win_size
    streamed = rounds == win_size and total // rounds == chan_size and per_shard == rounds
    stack_copies = (win_size, chan_size) if streamed else (win_size - 1,)
    ways = 2 if per_shard % 2 == 0 else 1
    count = per_shard // ways
    return pl.pallas_call(
        functools.partial(kernel, (chan_size, win_size, lag_blocks, windows, front), streamed, factor),
        out_shape=jax.ShapeDtypeStruct((per_win, channels, lag_count), jnp.float32),
        in_specs=[
            pl.BlockSpec(memory_space=pltpu.VMEM),
            pl.BlockSpec(memory_space=pltpu.SMEM),
            pl.BlockSpec(memory_space=pltpu.SMEM),
        ],
        out_specs=pl.BlockSpec(memory_space=pltpu.VMEM),
        scratch_shapes=[
            pltpu.VMEM((channels, (lag_blocks + 1) * BLOCK, inner), jnp.bfloat16),
            pltpu.VMEM((2, reach, BLOCK), jnp.bfloat16),
            pltpu.VMEM((ways, chan_size, count, depth, BLOCK), jnp.bfloat16),
            pltpu.VMEM((count, inner, ways * BLOCK), jnp.bfloat16),
            pltpu.VMEM((count, inner, ways * BLOCK), jnp.bfloat16),
            pltpu.VMEM((total, channels, lanes), jnp.float32),
            pltpu.VMEM((win_size, per_win, channels, lanes), jnp.float32),
            pltpu.VMEM((win_size - 1, per_win, channels, lanes), jnp.float32),
            pltpu.SemaphoreType.DMA((ways, chan_size - 1, count)),
            pltpu.SemaphoreType.DMA((ways, chan_size - 1, count)),
            pltpu.SemaphoreType.DMA(stack_copies),
            pltpu.SemaphoreType.DMA(stack_copies),
        ],
        compiler_params=pltpu.CompilerParams(
            vmem_limit_bytes=48 * 1024 * 1024, collective_id=0, has_side_effects=True
        ),
    )(pieces, local_channel, order)


def on_device(strain, sources):
    channels, windows, samples = strain.shape
    rounds, per_round = sources.shape
    total_sources = rounds * per_round
    factor = 1.0 / math.sqrt(lax.axis_size("win") * windows * samples)
    blocks = -(-samples // BLOCK)
    while blocks * windows % 16:
        blocks += 1
    depth = blocks * windows

    whitened = whiten(strain)
    padded = jnp.pad(whitened, ((0, 0), (0, 0), (0, blocks * BLOCK - samples)))
    pieces = padded.reshape(channels, windows, blocks, BLOCK)
    pieces = jnp.transpose(pieces, (0, 2, 1, 3)).reshape(channels, depth, BLOCK)

    flat_sources = sources.reshape(-1)
    per_shard = total_sources // lax.axis_size("chan")
    owner = flat_sources // channels
    position = jnp.arange(total_sources)
    earlier = (owner[None, :] == owner[:, None]) & (position[None, :] < position[:, None])
    rank = jnp.sum(earlier.astype(jnp.int32), axis=1)
    me = lax.axis_index("chan")
    mine = owner == me
    slot_pick = (mine[None, :] & (rank[None, :] == jnp.arange(per_shard)[:, None])).astype(jnp.int32)
    local_channel = jnp.sum(slot_pick * (flat_sources - me * channels)[None, :], axis=1)
    order = (owner * per_shard + rank).astype(jnp.int32)

    return correlate(pieces, local_channel.astype(jnp.int32), order, windows, rounds, factor)


def solution(mesh):
    in_specs = (P("chan", "win", None), P())
    out_specs = P("win", "chan", None)
    return jax.shard_map(
        on_device, mesh=mesh, in_specs=in_specs, out_specs=out_specs, check_vma=False
    )
```

profile of v0, /device:TPU:0, one launch (start us, length us, event | category | flops | bytes accessed | tf_op | source)
XLA Modules:
  0.0 54.1 jit_solution(4679575577701453426)
XLA Ops:
  0.0 0.0 copy-start
  0.0 1.9 %multiply_reduce_fusion = f32[8,8]{1,0:T(8,128)S(1)} fusion(f32[8,8,7500]{2,1,0:T(8,128)} %param.2), kind=kLoop, calls=%fused_computation.1 | loop fusion | flops 959936 | bytes 1920256 | tf_op jit(solution)/shard_map/reduce_sum | solution.py:16
  1.9 0.2 copy-done
  2.1 0.0 copy-start.1
  2.1 0.2 multiply_convert_fusion
  2.3 0.1 pad_bitcast_fusion.pieces_ref
  2.4 0.4 copy-done.1
  2.8 0.1 reshape.91
  2.9 0.2 convert_reduce_fusion
  3.1 0.1 select_reduce_fusion.local_ref
  3.2 50.2 %shard_map.28 = f32[8,8,513]{2,1,0:T(8,128)S(1)} custom-call(bf16[8,480,128]{2,1,0:T(8,128)(2,1)S(1)} %pad_bitcast_fusion.pieces_ref, s32[4]{0:T(128)S(1)} %select_reduce_fusion.local_ref, s32[32]{0:T(128)S(1)} %multiply_add_fusion.order_ref), custom_call_target="tpu_custom_call" | custom-call | tf_op jit(solution)/shard_map/pallas_call | solution.py:246
  53.4 0.7 %copy.4 = f32[8,8,513]{2,1,0:T(8,128)} copy(f32[8,8,513]{2,1,0:T(8,128)S(1)} %shard_map.28) | data formatting | bytes 262656
  (4 shorter events, 0.0 us)
Async XLA Ops:
  0.0 2.1 %copy-start = (f32[8,8,7500]{2,1,0:T(8,128)S(1)}, f32[8,8,7500]{2,1,0:T(8,128)}, u32[]{:S(2)}) copy-start(f32[8,8,7500]{2,1,0:T(8,128)} %param.2) | copy-start | bytes 5760004
  2.1 0.7 %copy-start.1 = (s32[4,8]{1,0:T(4,128)S(1)}, s32[4,8]{1,0:T(4,128)}, u32[]{:S(2)}) copy-start(s32[4,8]{1,0:T(4,128)} %param.3) | copy-start | bytes 388
where the time goes:
time: 54.3 us; the launch traced here: 54.1 us
  Pallas kernels  50.2 us (92%)
  other arithmetic  2.42 us (4%)
  local copies, waits for them, and re-layouts  1.44 us (3%)
    pallas_call x1, Pallas kernels, correlate(): pl.pallas_call(functools.partial(kernel, (chan_size, win_size, lag_blocks...  50.2 us
    reduce_sum x1, other arithmetic, whiten(): mean_square = jnp.mean(strain * strain, axis=-1, keepdims=True)  1.91 us
    unnamed x5, local copies, waits for them, and re-layouts  1.29 us

commit v1 on v0

--- a/solution.py
+++ b/solution.py
@@ -3,6 +3,8 @@
 
 import jax
 import jax.numpy as jnp
+import ml_dtypes
+import numpy as np
 from jax import lax
 from jax.experimental import pallas as pl
 from jax.experimental.pallas import tpu as pltpu
@@ -272,6 +274,467 @@
     )(pieces, local_channel, order)
 
 
+STEP = 32
+QUAD = BLOCK // STEP
+TAPS = MAX_LAG // STEP
+POINTS = 3 * TAPS
+TONES = POINTS // 2
+LAGS = 2 * MAX_LAG // STEP + 1
+HALO = MAX_LAG // BLOCK
+
+
+def tones():
+    return 2 * np.pi * (np.arange(TONES) + 0.5) / POINTS
+
+
+def wave_rows():
+    angle = np.outer(tones(), np.arange(POINTS))
+    rows = np.stack([np.cos(angle), -np.sin(angle)], axis=1)
+    scales = np.linspace(1.0, 2.0, 2000, endpoint=False)
+    kept, used = [], []
+    for row in rows:
+        scaled = scales[:, None, None] * row
+        near = scaled.astype(ml_dtypes.bfloat16).astype(np.float64)
+        error = np.sum((near / scales[:, None, None] - row) ** 2, axis=(1, 2))
+        best = int(np.argmin(error))
+        kept.append(near[best])
+        used.append(scales[best])
+    return np.array(kept), np.array(used)
+
+
+def constants(windows, channels, factor):
+    rows, scales = wave_rows()
+    bf16 = ml_dtypes.bfloat16
+    perm = np.zeros((QUAD, QUAD, STEP, QUAD, STEP, QUAD), np.float32)
+    for o in range(QUAD):
+        for q in range(QUAD):
+            perm[o, q, np.arange(STEP), q, np.arange(STEP), o] = 1
+    perm = perm.reshape(QUAD * BLOCK, QUAD * BLOCK)
+    parts = channels // QUAD
+    turn = np.zeros((STEP, parts, QUAD, parts, STEP, QUAD), np.float32)
+    for part in range(parts):
+        for c in range(QUAD):
+            turn[np.arange(STEP), part, c, part, np.arange(STEP), c] = 1
+    turn = turn.reshape(STEP * channels, STEP * channels)
+    eye = np.eye(windows)
+
+    def dft(taps):
+        blocks = (taps + TAPS) // QUAD
+        out = np.zeros((TONES, 2, 2, windows, QUAD, blocks, windows))
+        for seg in range(2):
+            for n in range(taps):
+                place = seg * TAPS + n
+                out[:, :, seg, :, place % QUAD, place // QUAD, :] = rows[:, :, n, None, None] * eye
+        return out.reshape(TONES * 4 * windows, QUAD * blocks * windows)
+
+    phase = np.repeat(np.outer(tones(), np.arange(STEP) / STEP), QUAD, axis=1)
+    twist = np.stack([np.cos(phase), np.sin(phase)], axis=1)
+    twist = np.broadcast_to(twist[:, :, None, :], (TONES, 2, 8, BLOCK))
+    angle = np.outer(np.arange(LAGS), tones())
+    back = np.stack([np.cos(angle), -np.sin(angle)], axis=2) * (factor / TONES / scales**2)[:, None]
+    inverse = np.einsum("kfv,cd->kcfvd", back, np.eye(channels)).reshape(LAGS * channels, TONES * 2 * channels)
+    return (
+        jnp.asarray(perm.astype(bf16)),
+        jnp.asarray(turn.astype(bf16)),
+        jnp.asarray(dft(TAPS).astype(bf16)),
+        jnp.asarray(dft(POINTS).astype(bf16)),
+        jnp.asarray(np.ascontiguousarray(twist).astype(np.float32)),
+        jnp.asarray(inverse.astype(np.float32)),
+    )
+
+
+def halves_kernel(
+    windows, pieces_ref, sources_ref, perm_ref, turn_ref, dft_a_ref, dft_b_ref, twist_ref, inverse_ref, out_ref,
+    pair_ref, own_ref, pick_ref, held_ref, xa_ref, sa_ref, a_ref, xb_ref, sb_ref, spec_ref, res_ref, land_ref,
+    half_ref, part_ref, fin_ref,
+    pair_sem, far_send, far_recv, side_send, side_recv, stack_send, stack_recv, end_sem,
+):
+    channels, depth, _ = pieces_ref.shape
+    rounds, per_round = sources_ref.shape
+    rows = held_ref.shape[3]
+    halo = HALO * windows
+    span = depth // 2
+    size = span + halo
+    pairs = sb_ref.shape[1] // 2 // (2 * windows)
+    two = 2 * windows
+    chan = lax.axis_index("chan")
+    win = lax.axis_index("win")
+    z, y = lax.div(chan, 2), lax.rem(chan, 2)
+    half = lax.rem(z, 2)
+    pair_z = z + 1 - 2 * half
+    far = [lax.rem(z - half + 2 + k, QUAD) for k in range(2)]
+    order = [z, pair_z] + far
+    MESH = pl.DeviceIdType.MESH
+
+    def source_rows(h):
+        return pl.ds(pl.multiple_of(h * (span - halo), 16), size)
+
+    def held_rows(h):
+        return pl.ds(pl.multiple_of((1 - h) * halo, 16), size)
+
+    def round_at(step):
+        return lax.rem(win + 1 + step, rounds)
+
+    def channel_of(step, shard):
+        found = jnp.int32(0)
+        for i in range(per_round):
+            source = sources_ref[round_at(step), i]
+            found += jnp.where(source // channels == shard, source - shard * channels, 0)
+        return found
+
+    barrier = pltpu.get_barrier_semaphore()
+    edge = jnp.zeros((16, BLOCK), jnp.bfloat16)
+    edges = [*range(0, halo, 16), *range(size, rows, 16)]
+    for at in edges:
+        for step in range(rounds):
+            for side in range(2):
+                for zz in range(QUAD):
+                    held_ref[step, side, zz, at : at + 16, :] = edge
+        for c in range(channels):
+            pair_ref[c, at : at + 16, :] = edge
+            own_ref[c, at : at + 16, :] = edge
+    peers = [{"chan": pair_z * 2 + y}, {"chan": far[0] * 2 + y}, {"chan": far[1] * 2 + y}, {"chan": z * 2 + 1 - y}]
+    peers += [{"win": lax.rem(win + 1 + step, rounds)} for step in range(rounds - 1)]
+    for peer in peers:
+        pl.semaphore_signal(barrier, inc=1, device_id=peer, device_id_type=MESH)
+
+    pair_copy = pltpu.make_async_remote_copy(
+        src_ref=pieces_ref.at[:, source_rows(1 - half), :],
+        dst_ref=pair_ref.at[:, held_rows(1 - half), :],
+        send_sem=pair_sem.at[0],
+        recv_sem=pair_sem.at[1],
+        device_id=peers[0],
+        device_id_type=MESH,
+    )
+
+    def far_copy(step, k):
+        return pltpu.make_async_remote_copy(
+            src_ref=pick_ref.at[step, source_rows(k), :],
+            dst_ref=held_ref.at[step, 0, z, held_rows(k), :],
+            send_sem=far_send.at[step, k],
+            recv_sem=far_recv.at[step, half],
+            device_id=peers[1 + k],
+            device_id_type=MESH,
+        )
+
+    def far_wait(step, k):
+        pltpu.make_async_remote_copy(
+            src_ref=pick_ref.at[step, source_rows(half), :],
+            dst_ref=held_ref.at[step, 0, far[k], held_rows(half), :],
+            send_sem=far_send.at[step, k],
+            recv_sem=far_recv.at[step, k],
+            device_id=peers[1 + k],
+            device_id_type=MESH,
+        ).wait_recv()
+
+    def side_copy(step, o):
+        return pltpu.make_async_remote_copy(
+            src_ref=held_ref.at[step, 0, order[o], held_rows(half), :],
+            dst_ref=held_ref.at[step, 1, order[o], held_rows(half), :],
+            send_sem=side_send.at[step, o],
+            recv_sem=side_recv.at[step, o],
+            device_id=peers[3],
+            device_id_type=MESH,
+        )
+
+    def stack_copy(step):
+        return pltpu.make_async_remote_copy(
+            src_ref=res_ref.at[step],
+            dst_ref=land_ref.at[step],
+            send_sem=stack_send.at[step],
+            recv_sem=stack_recv.at[step],
+            device_id={"win": lax.rem(win + 1 + step, rounds)},
+            device_id_type=MESH,
+        )
+
+    end_copy = pltpu.make_async_remote_copy(
+        src_ref=half_ref,
+        dst_ref=part_ref,
+        send_sem=end_sem.at[0],
+        recv_sem=end_sem.at[1],
+        device_id=peers[0],
+        device_id_type=MESH,
+    )
+
+    for step in range(rounds):
+        pick_ref[step] = pieces_ref[channel_of(step, chan)]
+        held_ref[step, 0, z, held_rows(half), :] = pick_ref[step, source_rows(half), :]
+    for c in range(channels):
+        own_ref[c, held_rows(half), :] = pieces_ref[c, source_rows(half), :]
+    pl.semaphore_wait(barrier, len(peers))
+    for k in range(2):
+        far_copy(0, k).start()
+    pair_copy.start()
+    for step in range(rounds):
+        side_copy(step, 0).start()
+        if step:
+            for k in range(2):
+                far_copy(step, k).start()
+
+    def twisted(real, imag, f):
+        cos, sin = twist_ref[f, 0], twist_ref[f, 1]
+        reals, imags = [], []
+        for part in range(real.shape[1] // BLOCK):
+            lanes = slice(part * BLOCK, (part + 1) * BLOCK)
+            turned = []
+            for at in range(0, real.shape[0], 8):
+                re, im = real[at : at + 8, lanes], imag[at : at + 8, lanes]
+                turned.append((re * cos + im * sin, im * cos - re * sin))
+            reals.append(jnp.concatenate([t[0] for t in turned], axis=0))
+            imags.append(jnp.concatenate([t[1] for t in turned], axis=0))
+        return jnp.concatenate(reals, axis=1).astype(jnp.bfloat16), jnp.concatenate(imags, axis=1).astype(jnp.bfloat16)
+
+    def spread(refs, at, count, put):
+        joined = jnp.concatenate([r[at : at + count, :] for r in refs], axis=1)
+        put(jnp.dot(joined, perm_ref[...], preferred_element_type=jnp.float32).astype(jnp.bfloat16))
+
+    def receivers(which, ref):
+        for part in range(channels // QUAD):
+            def put(value):
+                for q in range(QUAD):
+                    xa_ref[q, 0:span, part * BLOCK : (part + 1) * BLOCK] = value[:, q * BLOCK : (q + 1) * BLOCK]
+
+            spread([ref.at[part * QUAD + o] for o in range(QUAD)], halo, span, put)
+
+        def waves(g, carry):
+            at = pl.multiple_of(g * two * TAPS // QUAD, 16)
+            taken = jnp.concatenate([xa_ref[q, pl.ds(at, two * TAPS // QUAD), :] for q in range(QUAD)], axis=0)
+            seen = jnp.dot(dft_a_ref[...], taken, preferred_element_type=jnp.float32)
+            here = pl.multiple_of(g * two, 16)
+            for f in range(TONES):
+                real, imag = twisted(seen[2 * f * two : (2 * f + 1) * two], seen[(2 * f + 1) * two : (2 * f + 2) * two], f)
+                sa_ref[f, 0, pl.ds(here, two), :] = real
+                sa_ref[f, 1, pl.ds(here, two), :] = imag
+            return carry
+
+        lax.fori_loop(0, pairs, waves, 0)
+        wide = pairs * two
+
+        def turned(f, carry):
+            real, imag = [
+                lax.dot_general(
+                    turn_ref[...], sa_ref[f, v], (((1,), (1,)), ((), ())), preferred_element_type=jnp.float32
+                ).astype(jnp.bfloat16)
+                for v in range(2)
+            ]
+            a_ref[which, f, 0, :, 0:wide] = real
+            a_ref[which, f, 0, :, wide : 2 * wide] = imag
+            a_ref[which, f, 1, :, 0:wide] = -imag
+            a_ref[which, f, 1, :, wide : 2 * wide] = real
+            return carry
+
+        lax.fori_loop(0, TONES, turned, 0)
+
+    def sources(step):
+        wide = pairs * two
+        for side in range(2):
+            def put(value):
+                for q in range(QUAD):
+                    xb_ref[q, :, side * BLOCK : (side + 1) * BLOCK] = value[:, q * BLOCK : (q + 1) * BLOCK]
+
+            spread([held_ref.at[step, side, zz] for zz in range(QUAD)], 0, rows, put)
+
+        def waves(g, carry):
+            count = windows * (TAPS + POINTS) // QUAD
+            at = pl.multiple_of(g * two * TAPS // QUAD, 16)
+            taken = jnp.concatenate([xb_ref[q, pl.ds(at, count), :] for q in range(QUAD)], axis=0)
+            seen = jnp.dot(dft_b_ref[...], taken, preferred_element_type=jnp.float32)
+            here = pl.multiple_of(g * two, 16)
+            for f in range(TONES):
+                real, imag = twisted(seen[2 * f * two : (2 * f + 1) * two], seen[(2 * f + 1) * two : (2 * f + 2) * two], f)
+                sb_ref[f, pl.ds(here, two), :] = real
+                sb_ref[f, pl.ds(pl.multiple_of(here + wide, 16), two), :] = imag
+            return carry
+
+        lax.fori_loop(0, pairs, waves, 0)
+
+    def products(step):
+        def tone(f, carry):
+            right = sb_ref[f]
+            for which in range(2):
+                sums = []
+                for v in range(2):
+                    seen = jnp.dot(a_ref[which, f, v], right, preferred_element_type=jnp.float32)
+                    for side in range(2):
+                        lanes = slice(side * BLOCK, (side + 1) * BLOCK)
+                        total = [None] * 4
+                        for i in range(STEP):
+                            term = seen[i * channels : (i + 1) * channels, lanes]
+                            if i:
+                                term = pltpu.roll(term, BLOCK - QUAD * i, 1)
+                            total[i % 4] = term if total[i % 4] is None else total[i % 4] + term
+                        sums.append((total[0] + total[1]) + (total[2] + total[3]))
+                cos, sin = twist_ref[f, 0], twist_ref[f, 1]
+                at = pl.multiple_of(f * 2 * channels, 16)
+                for side in range(2):
+                    lanes = slice(side * BLOCK, (side + 1) * BLOCK)
+                    re, im = sums[side], sums[2 + side]
+                    both = jnp.concatenate([re * cos - im * sin, re * sin + im * cos], axis=0)
+                    spec_ref[which, pl.ds(at, 2 * channels), lanes] = both
+            return carry
+
+        lax.fori_loop(0, TONES, tone, 0)
+        for which in range(2):
+            res_ref[step, which] = jnp.dot(
+                inverse_ref[...], spec_ref[which], precision=lax.Precision.HIGHEST, preferred_element_type=jnp.float32
+            )
+
+    xa_ref[:, span:, :] = jnp.zeros((QUAD, xa_ref.shape[1] - span, xa_ref.shape[2]), jnp.bfloat16)
+    receivers(0, own_ref)
+    pair_copy.wait_recv()
+    for step in range(rounds):
+        channel = channel_of(step, pair_z * 2 + y)
+        held_ref[step, 0, pair_z, held_rows(half), :] = pair_ref[channel, held_rows(half), :]
+        side_copy(step, 1).start()
+    receivers(1, pair_ref)
+
+    def pass_on(step):
+        for k in range(2):
+            far_wait(step, k)
+            side_copy(step, 2 + k).start()
+
+    pass_on(0)
+
+    def body(step, carry):
+        for o in range(QUAD):
+            side_copy(step, o).wait_recv()
+        sources(step)
+
+        @pl.when(step < rounds - 1)
+        def _():
+            pass_on(step + 1)
+
+        products(step)
+
+        @pl.when(step < rounds - 1)
+        def _():
+            stack_copy(step).start()
+
+        return carry
+
+    lax.fori_loop(0, rounds, body, 0)
+
+    for step in range(rounds - 1):
+        stack_copy(step).wait_recv()
+    sums = []
+    for which in range(2):
+        total = res_ref[rounds - 1, which]
+        for step in range(rounds - 1):
+            total = total + land_ref[step, which]
+        if which == 0:
+            sums.append(total)
+        else:
+            half_ref[...] = total
+    end_copy.start()
+    for step in range(rounds):
+        for k in range(2):
+            far_copy(step, k).wait_send()
+        for o in range(QUAD):
+            side_copy(step, o).wait_send()
+    pair_copy.wait_send()
+    for step in range(rounds - 1):
+        stack_copy(step).wait_send()
+    end_copy.wait_recv()
+    total = sums[0] + part_ref[...]
+    groups = (LAGS - 1) // QUAD
+    for side in range(2):
+        lanes = slice(side * BLOCK, (side + 1) * BLOCK)
+        lined = jnp.concatenate(
+            [
+                jnp.concatenate(
+                    [total[(QUAD * g + q) * channels : (QUAD * g + q + 1) * channels, lanes] for g in range(groups)], axis=0
+                )
+                for q in range(QUAD)
+            ],
+            axis=1,
+        )
+        high = lined.astype(jnp.bfloat16)
+        rest = lined - high.astype(jnp.float32)
+        middle = rest.astype(jnp.bfloat16)
+        low = (rest - middle.astype(jnp.float32)).astype(jnp.bfloat16)
+        split = [
+            lax.dot_general(p, perm_ref[...], (((1,), (1,)), ((), ())), preferred_element_type=jnp.float32)
+            for p in (high, middle, low)
+        ]
+        whole = split[0] + split[1] + split[2]
+        last = total[(LAGS - 1) * channels : LAGS * channels, lanes]
+        for zz in range(QUAD):
+            for g in range(groups):
+                fin_ref[side * QUAD + zz, :, g * BLOCK : (g + 1) * BLOCK] = whole[
+                    g * channels : (g + 1) * channels, zz * BLOCK : (zz + 1) * BLOCK
+                ]
+            fin_ref[side * QUAD + zz, :, groups * BLOCK : (groups + 1) * BLOCK] = jnp.broadcast_to(
+                last[:, zz : zz + 1], (channels, BLOCK)
+            )
+    for i in range(per_round):
+        shard = sources_ref[win, i] // channels
+        side = jnp.where(shard - 2 * (shard // 2) == y, 0, 1)
+        out_ref[i] = fin_ref[side * QUAD + shard // 2][:, : out_ref.shape[2]]
+    end_copy.wait_send()
+
+
+def halves_fit(channels, windows, blocks, rounds, per_round):
+    chan_size, win_size = lax.axis_size("chan"), lax.axis_size("win")
+    return (
+        rounds == win_size
+        and per_round == chan_size
+        and chan_size == 2 * QUAD
+        and win_size == QUAD
+        and channels == 2 * QUAD
+        and windows == 8
+        and blocks % 4 == 0
+    )
+
+
+def correlate_halves(pieces, sources, factor):
+    channels, depth, _ = pieces.shape
+    rounds, per_round = sources.shape
+    windows = 8
+    tables = constants(windows, channels, factor)
+    span = depth // 2
+    pairs = -(-span // (windows * 4))
+    rows = (pairs * 4 + 2 * HALO) * windows
+    wide = channels * STEP
+    stack = (LAGS * channels, 2 * BLOCK)
+    bf16, f32 = jnp.bfloat16, jnp.float32
+    dma = pltpu.SemaphoreType.DMA
+    return pl.pallas_call(
+        functools.partial(halves_kernel, windows),
+        out_shape=jax.ShapeDtypeStruct((per_round, channels, 2 * MAX_LAG + 1), f32),
+        in_specs=[pl.BlockSpec(memory_space=pltpu.VMEM), pl.BlockSpec(memory_space=pltpu.SMEM)]
+        + [pl.BlockSpec(memory_space=pltpu.VMEM)] * len(tables),
+        out_specs=pl.BlockSpec(memory_space=pltpu.VMEM),
+        scratch_shapes=[
+            pltpu.VMEM((channels, rows, BLOCK), bf16),
+            pltpu.VMEM((channels, rows, BLOCK), bf16),
+            pltpu.VMEM((rounds, depth, BLOCK), bf16),
+            pltpu.VMEM((rounds, 2, QUAD, rows, BLOCK), bf16),
+            pltpu.VMEM((QUAD, pairs * 4 * windows, wide), bf16),
+            pltpu.VMEM((TONES, 2, pairs * 2 * windows, wide), bf16),
+            pltpu.VMEM((2, TONES, 2, wide, pairs * 4 * windows), bf16),
+            pltpu.VMEM((QUAD, rows, 2 * BLOCK), bf16),
+            pltpu.VMEM((TONES, pairs * 4 * windows, 2 * BLOCK), bf16),
+            pltpu.VMEM((2, TONES * 2 * channels, 2 * BLOCK), f32),
+            pltpu.VMEM((rounds, 2, *stack), f32),
+            pltpu.VMEM((rounds - 1, 2, *stack), f32),
+            pltpu.VMEM(stack, f32),
+            pltpu.VMEM(stack, f32),
+            pltpu.VMEM((per_round, channels, 2 * MAX_LAG + BLOCK), f32),
+            dma((2,)),
+            dma((rounds, 2)),
+            dma((rounds, 2)),
+            dma((rounds, QUAD)),
+            dma((rounds, QUAD)),
+            dma((rounds - 1,)),
+            dma((rounds - 1,)),
+            dma((2,)),
+        ],
+        compiler_params=pltpu.CompilerParams(
+            vmem_limit_bytes=48 * 1024 * 1024, collective_id=1, has_side_effects=True
+        ),
+    )(pieces, sources, *tables)
+
+
 def on_device(strain, sources):
     channels, windows, samples = strain.shape
     rounds, per_round = sources.shape
@@ -286,6 +749,9 @@
     padded = jnp.pad(whitened, ((0, 0), (0, 0), (0, blocks * BLOCK - samples)))
     pieces = padded.reshape(channels, windows, blocks, BLOCK)
     pieces = jnp.transpose(pieces, (0, 2, 1, 3)).reshape(channels, depth, BLOCK)
+
+    if halves_fit(channels, windows, blocks, rounds, per_round):
+        return correlate_halves(pieces, sources.astype(jnp.int32), factor)
 
     flat_sources = sources.reshape(-1)
     per_shard = total_sources // lax.axis_size("chan")

time: 54.3 us -> 83.1 us (1.53)
  the two profiles are of different devices: /device:TPU:0 before, /device:TPU:10 now
where the time goes in v1:
time: 83.1 us; the launch traced here: 83 us
  Pallas kernels  79 us (95%)
  other arithmetic  2.1 us (3%)
  local copies, waits for them, and re-layouts  1.86 us (2%)
    pallas_call x1, Pallas kernels, correlate_halves(): pl.pallas_call(functools.partial(halves_kernel, windows), out_shape=jax.S...  79 us
    reduce_sum x1, other arithmetic, whiten(): mean_square = jnp.mean(strain * strain, axis=-1, keepdims=True)  1.91 us
    unnamed x17, local copies, waits for them, and re-layouts  1.8 us

profile of v1, /device:TPU:10, one launch (start us, length us, event | category | flops | bytes accessed | tf_op | source)
XLA Modules:
  0.0 83.0 jit_solution(16326280403540439328)
XLA Ops:
  0.0 0.0 copy-start.7
  0.0 1.9 %multiply_reduce_fusion = f32[8,8]{1,0:T(8,128)S(1)} fusion(f32[8,8,7500]{2,1,0:T(8,128)} %param.8), kind=kLoop, calls=%fused_computation.1 | loop fusion | flops 959936 | bytes 1920256 | tf_op jit(solution)/shard_map/reduce_sum | solution.py:18
  1.9 0.2 copy-done.7
  2.1 0.0 copy-start
  2.1 0.0 copy-start.1
  2.1 0.0 copy-start.2
  2.1 0.0 copy-start.3
  2.1 0.0 copy-start.4
  2.1 0.0 copy-start.5
  2.2 0.0 copy-start.6
  2.2 0.2 multiply_convert_fusion
  2.3 0.1 pad_bitcast_fusion.pieces_ref
  2.4 0.7 copy-done
  3.2 0.0 copy-done.1
  3.2 0.0 copy-done.2
  3.2 0.0 copy-done.3
  3.3 0.0 copy-done.4
  3.3 0.0 copy-done.5
  3.3 0.0 copy-done.6
  3.3 79.0 %shard_map.82 = f32[8,8,513]{2,1,0:T(8,128)S(1)} custom-call(bf16[8,480,128]{2,1,0:T(8,128)(2,1)S(1)} %pad_bitcast_fusion.pieces_ref, s32[4,8]{1,0:T(4,128)S(1)} %copy-done.6, bf16[512,512]{1,0:T(8,128)(2,1)S(1)} %copy-done, bf16[256,256]{1,0:T(8,128)(2,1)S(1)} %copy-done.3, bf16[384,128]{1,0:T(8,128)(2,1)S(1)} %copy-done.5, bf16[384,256]{1,0:T(8,128)(2,1)S(1)} %copy-done.1, ...), custom_call_target="tpu_custom_call" | custom-call | tf_op jit(solution)/shard_map/pallas_call | solution.py:701
  82.3 0.7 copy.10
  (1 shorter events, 0.0 us)
Async XLA Ops:
  0.0 2.1 %copy-start.7 = (f32[8,8,7500]{2,1,0:T(8,128)S(1)}, f32[8,8,7500]{2,1,0:T(8,128)}, u32[]{:S(2)}) copy-start(f32[8,8,7500]{2,1,0:T(8,128)} %param.8) | copy-start | bytes 5760004
  2.1 1.0 %copy-start = (bf16[512,512]{1,0:T(8,128)(2,1)S(1)}, bf16[512,512]{1,0:T(8,128)(2,1)}, u32[]{:S(2)}) copy-start(bf16[512,512]{1,0:T(8,128)(2,1)} %constant.22.clone.perm_ref) | copy-start | bytes 1572868
  2.1 1.1 %copy-start.1 = (bf16[384,256]{1,0:T(8,128)(2,1)S(1)}, bf16[384,256]{1,0:T(8,128)(2,1)}, u32[]{:S(2)}) copy-start(bf16[384,256]{1,0:T(8,128)(2,1)} %constant.25.clone.dft_b_ref) | copy-start | bytes 589828
  2.1 1.1 %copy-start.2 = (f32[136,192]{1,0:T(8,128)S(1)}, f32[136,192]{1,0:T(8,128)}, u32[]{:S(2)}) copy-start(f32[136,192]{1,0:T(8,128)} %constant.27.clone.inverse_ref) | copy-start | bytes 313348
  2.1 1.2 %copy-start.3 = (bf16[256,256]{1,0:T(8,128)(2,1)S(1)}, bf16[256,256]{1,0:T(8,128)(2,1)}, u32[]{:S(2)}) copy-start(bf16[256,256]{1,0:T(8,128)(2,1)} %constant.23.clone.turn_ref) | copy-start | bytes 393220
  2.1 1.2 %copy-start.4 = (f32[12,2,8,128]{3,2,1,0:T(8,128)S(1)}, f32[12,2,8,128]{3,2,1,0:T(8,128)}, u32[]{:S(2)}) copy-start(f32[12,2,8,128]{3,2,1,0:T(8,128)} %constant.26.clone.twist_ref) | copy-start | bytes 294916
  2.1 1.2 %copy-start.5 = (bf16[384,128]{1,0:T(8,128)(2,1)S(1)}, bf16[384,128]{1,0:T(8,128)(2,1)}, u32[]{:S(2)}) copy-start(bf16[384,128]{1,0:T(8,128)(2,1)} %constant.24.clone.dft_a_ref) | copy-start | bytes 294916
  2.2 1.2 %copy-start.6 = (s32[4,8]{1,0:T(4,128)S(1)}, s32[4,8]{1,0:T(4,128)}, u32[]{:S(2)}) copy-start(s32[4,8]{1,0:T(4,128)} %sources_ref.1) | copy-start | bytes 388

commit v2 on v1

--- a/solution.py
+++ b/solution.py
@@ -345,7 +345,7 @@
 
 def halves_kernel(
     windows, pieces_ref, sources_ref, perm_ref, turn_ref, dft_a_ref, dft_b_ref, twist_ref, inverse_ref, out_ref,
-    pair_ref, own_ref, pick_ref, held_ref, xa_ref, sa_ref, a_ref, xb_ref, sb_ref, spec_ref, res_ref, land_ref,
+    near_ref, pair_ref, own_ref, pick_ref, held_ref, spun_ref, xa_ref, sa_ref, a_ref, xb_ref, sb_ref, spec_ref, res_ref, sent_ref, land_ref,
     half_ref, part_ref, fin_ref,
     pair_sem, far_send, far_recv, side_send, side_recv, stack_send, stack_recv, end_sem,
 ):
@@ -355,7 +355,7 @@
     halo = HALO * windows
     span = depth // 2
     size = span + halo
-    pairs = sb_ref.shape[1] // 2 // (2 * windows)
+    pairs = sb_ref.shape[2] // 4 // (2 * windows)
     two = 2 * windows
     chan = lax.axis_index("chan")
     win = lax.axis_index("win")
@@ -373,7 +373,7 @@
         return pl.ds(pl.multiple_of((1 - h) * halo, 16), size)
 
     def round_at(step):
-        return lax.rem(win + 1 + step, rounds)
+        return lax.rem(win + jnp.where(step == 0, 2, jnp.where(step == 1, 1, jnp.where(step == 2, 3, 0))), rounds)
 
     def channel_of(step, shard):
         found = jnp.int32(0)
@@ -381,6 +381,35 @@
             source = sources_ref[round_at(step), i]
             found += jnp.where(source // channels == shard, source - shard * channels, 0)
         return found
+
+    def plan(shard):
+        wanted = [channel_of(step, shard) for step in range(rounds)]
+        first = []
+        for step in range(rounds):
+            found = jnp.int32(step)
+            for earlier in reversed(range(step)):
+                found = jnp.where(wanted[earlier] == wanted[step], earlier, found)
+            first.append(found)
+        ranks, free = [], jnp.int32(0)
+        for c in range(channels):
+            taken = jnp.int32(0)
+            for channel in wanted:
+                taken = jnp.where(channel == c, 1, taken)
+            ranks.append(jnp.where(taken == 1, -1, free))
+            free = free + 1 - taken
+        line, spare = [], jnp.int32(0)
+        for place in range(channels):
+            filler = jnp.int32(0)
+            for c in range(channels):
+                filler = jnp.where(ranks[c] == spare, c, filler)
+            if place < rounds:
+                repeated = jnp.where(first[place] == place, 0, 1)
+                line.append(jnp.where(repeated == 1, filler, wanted[place]))
+                spare = spare + repeated
+            else:
+                line.append(filler)
+                spare = spare + 1
+        return wanted, first, line
 
     barrier = pltpu.get_barrier_semaphore()
     edge = jnp.zeros((16, BLOCK), jnp.bfloat16)
@@ -398,14 +427,25 @@
     for peer in peers:
         pl.semaphore_signal(barrier, inc=1, device_id=peer, device_id_type=MESH)
 
-    pair_copy = pltpu.make_async_remote_copy(
-        src_ref=pieces_ref.at[:, source_rows(1 - half), :],
-        dst_ref=pair_ref.at[:, held_rows(1 - half), :],
-        send_sem=pair_sem.at[0],
-        recv_sem=pair_sem.at[1],
-        device_id=peers[0],
-        device_id_type=MESH,
-    )
+    def near_copy(place):
+        return pltpu.make_async_remote_copy(
+            src_ref=near_ref.at[place],
+            dst_ref=pair_ref.at[place, held_rows(1 - half), :],
+            send_sem=pair_sem.at[0, place],
+            recv_sem=pair_sem.at[1, place],
+            device_id=peers[0],
+            device_id_type=MESH,
+        )
+
+    def near_wait(place):
+        pltpu.make_async_remote_copy(
+            src_ref=near_ref.at[place],
+            dst_ref=pair_ref.at[place, held_rows(half), :],
+            send_sem=pair_sem.at[0, place],
+            recv_sem=pair_sem.at[1, place],
+            device_id=peers[0],
+            device_id_type=MESH,
+        ).wait_recv()
 
     def far_copy(step, k):
         return pltpu.make_async_remote_copy(
@@ -437,13 +477,13 @@
             device_id_type=MESH,
         )
 
-    def stack_copy(step):
+    def stack_copy(step, which):
         return pltpu.make_async_remote_copy(
-            src_ref=res_ref.at[step],
-            dst_ref=land_ref.at[step],
-            send_sem=stack_send.at[step],
-            recv_sem=stack_recv.at[step],
-            device_id={"win": lax.rem(win + 1 + step, rounds)},
+            src_ref=sent_ref.at[step, which],
+            dst_ref=land_ref.at[step, which],
+            send_sem=stack_send.at[step, which],
+            recv_sem=stack_recv.at[step, which],
+            device_id={"win": round_at(step)},
             device_id_type=MESH,
         )
 
@@ -456,20 +496,25 @@
         device_id_type=MESH,
     )
 
+    wanted, _, line = plan(chan)
     for step in range(rounds):
-        pick_ref[step] = pieces_ref[channel_of(step, chan)]
+        pick_ref[step] = pieces_ref[wanted[step]]
         held_ref[step, 0, z, held_rows(half), :] = pick_ref[step, source_rows(half), :]
+    for place in range(channels):
+        near_ref[place] = pieces_ref[line[place], source_rows(1 - half), :]
+    pl.semaphore_wait(barrier, len(peers))
+    ahead = [1, 2, 5, 8]
+    sent = 0
+    for step in range(rounds):
+        for place in range(sent, ahead[step]):
+            near_copy(place).start()
+        sent = ahead[step]
+        for k in range(2):
+            far_copy(step, k).start()
+    for step in range(rounds):
+        side_copy(step, 0).start()
     for c in range(channels):
         own_ref[c, held_rows(half), :] = pieces_ref[c, source_rows(half), :]
-    pl.semaphore_wait(barrier, len(peers))
-    for k in range(2):
-        far_copy(0, k).start()
-    pair_copy.start()
-    for step in range(rounds):
-        side_copy(step, 0).start()
-        if step:
-            for k in range(2):
-                far_copy(step, k).start()
 
     def twisted(real, imag, f):
         cos, sin = twist_ref[f, 0], twist_ref[f, 1]
@@ -484,11 +529,14 @@
             imags.append(jnp.concatenate([t[1] for t in turned], axis=0))
         return jnp.concatenate(reals, axis=1).astype(jnp.bfloat16), jnp.concatenate(imags, axis=1).astype(jnp.bfloat16)
 
+    def half_turn(value):
+        return pltpu.roll(value, BLOCK // 2, 1)
+
     def spread(refs, at, count, put):
         joined = jnp.concatenate([r[at : at + count, :] for r in refs], axis=1)
         put(jnp.dot(joined, perm_ref[...], preferred_element_type=jnp.float32).astype(jnp.bfloat16))
 
-    def receivers(which, ref):
+    def receivers(which, ref, spin_ref):
         for part in range(channels // QUAD):
             def put(value):
                 for q in range(QUAD):
@@ -507,23 +555,27 @@
                 sa_ref[f, 1, pl.ds(here, two), :] = imag
             return carry
 
-        lax.fori_loop(0, pairs, waves, 0)
+        lax.fori_loop(0, pairs, waves, 0, unroll=8)
         wide = pairs * two
 
         def turned(f, carry):
             real, imag = [
                 lax.dot_general(
-                    turn_ref[...], sa_ref[f, v], (((1,), (1,)), ((), ())), preferred_element_type=jnp.float32
+                    spin_ref[...], sa_ref[f, v], (((1,), (1,)), ((), ())), preferred_element_type=jnp.float32
                 ).astype(jnp.bfloat16)
                 for v in range(2)
             ]
-            a_ref[which, f, 0, :, 0:wide] = real
-            a_ref[which, f, 0, :, wide : 2 * wide] = imag
-            a_ref[which, f, 1, :, 0:wide] = -imag
-            a_ref[which, f, 1, :, wide : 2 * wide] = real
+            deep = STEP * channels // 2
+            for u in range(2):
+                at = 2 * u * wide
+                re, im = real[u * deep : (u + 1) * deep], imag[u * deep : (u + 1) * deep]
+                a_ref[which, f, 0, :, at : at + wide] = re
+                a_ref[which, f, 0, :, at + wide : at + 2 * wide] = im
+                a_ref[which, f, 1, :, at : at + wide] = -im
+                a_ref[which, f, 1, :, at + wide : at + 2 * wide] = re
             return carry
 
-        lax.fori_loop(0, TONES, turned, 0)
+        lax.fori_loop(0, TONES, turned, 0, unroll=12)
 
     def sources(step):
         wide = pairs * two
@@ -542,107 +594,152 @@
             here = pl.multiple_of(g * two, 16)
             for f in range(TONES):
                 real, imag = twisted(seen[2 * f * two : (2 * f + 1) * two], seen[(2 * f + 1) * two : (2 * f + 2) * two], f)
-                sb_ref[f, pl.ds(here, two), :] = real
-                sb_ref[f, pl.ds(pl.multiple_of(here + wide, 16), two), :] = imag
-            return carry
-
-        lax.fori_loop(0, pairs, waves, 0)
-
-    def products(step):
-        def tone(f, carry):
-            right = sb_ref[f]
-            for which in range(2):
-                sums = []
-                for v in range(2):
-                    seen = jnp.dot(a_ref[which, f, v], right, preferred_element_type=jnp.float32)
+                for v, part in enumerate((real, imag)):
+                    sb_ref[step, f, pl.ds(pl.multiple_of(here + v * wide, 16), two), :] = part
                     for side in range(2):
                         lanes = slice(side * BLOCK, (side + 1) * BLOCK)
-                        total = [None] * 4
-                        for i in range(STEP):
-                            term = seen[i * channels : (i + 1) * channels, lanes]
-                            if i:
-                                term = pltpu.roll(term, BLOCK - QUAD * i, 1)
-                            total[i % 4] = term if total[i % 4] is None else total[i % 4] + term
-                        sums.append((total[0] + total[1]) + (total[2] + total[3]))
-                cos, sin = twist_ref[f, 0], twist_ref[f, 1]
-                at = pl.multiple_of(f * 2 * channels, 16)
+                        sb_ref[step, f, pl.ds(pl.multiple_of(here + (v + 2) * wide, 16), two), lanes] = half_turn(part[:, lanes])
+            return carry
+
+        lax.fori_loop(0, pairs, waves, 0, unroll=8)
+
+    def products(step, which):
+        def tone(f, carry):
+            right = sb_ref[step, f]
+            sums = []
+            for v in range(2):
+                seen = jnp.dot(a_ref[which, f, v], right, preferred_element_type=jnp.float32)
                 for side in range(2):
                     lanes = slice(side * BLOCK, (side + 1) * BLOCK)
-                    re, im = sums[side], sums[2 + side]
-                    both = jnp.concatenate([re * cos - im * sin, re * sin + im * cos], axis=0)
-                    spec_ref[which, pl.ds(at, 2 * channels), lanes] = both
+                    total = [None] * 4
+                    for i in range(STEP // 2):
+                        term = seen[i * channels : (i + 1) * channels, lanes]
+                        if i:
+                            term = pltpu.roll(term, BLOCK - QUAD * i, 1)
+                        total[i % 4] = term if total[i % 4] is None else total[i % 4] + term
+                    sums.append((total[0] + total[1]) + (total[2] + total[3]))
+            cos, sin = twist_ref[f, 0], twist_ref[f, 1]
+            at = pl.multiple_of(f * 2 * channels, 16)
+            for side in range(2):
+                lanes = slice(side * BLOCK, (side + 1) * BLOCK)
+                re, im = sums[side], sums[2 + side]
+                both = jnp.concatenate([re * cos - im * sin, re * sin + im * cos], axis=0)
+                spec_ref[which, pl.ds(at, 2 * channels), lanes] = both
             return carry
 
-        lax.fori_loop(0, TONES, tone, 0)
-        for which in range(2):
-            res_ref[step, which] = jnp.dot(
-                inverse_ref[...], spec_ref[which], precision=lax.Precision.HIGHEST, preferred_element_type=jnp.float32
-            )
-
-    xa_ref[:, span:, :] = jnp.zeros((QUAD, xa_ref.shape[1] - span, xa_ref.shape[2]), jnp.bfloat16)
-    receivers(0, own_ref)
-    pair_copy.wait_recv()
-    for step in range(rounds):
-        channel = channel_of(step, pair_z * 2 + y)
-        held_ref[step, 0, pair_z, held_rows(half), :] = pair_ref[channel, held_rows(half), :]
+        lax.fori_loop(0, TONES, tone, 0, unroll=12)
+        sums = jnp.dot(
+            inverse_ref[...], spec_ref[which], precision=lax.Precision.HIGHEST, preferred_element_type=jnp.float32
+        )
+        sums = jnp.concatenate([sums[:, :BLOCK], sums[:, BLOCK:]], axis=0)
+        res_ref[which] = sums
+        sent_ref[step, which] = sums.astype(jnp.bfloat16)
+
+    _, first, pair_line = plan(pair_z * 2 + y)
+
+    def pass_on(step):
+        if step < 3:
+            near_wait(step)
+        total = pair_ref[0, held_rows(half), :]
+        if step:
+            total = jnp.zeros(total.shape, jnp.float32)
+            for place in range(step + 1):
+                share = jnp.where(first[step] == place, 1.0, 0.0)
+                total = total + pair_ref[place, held_rows(half), :].astype(jnp.float32) * share
+            total = total.astype(jnp.bfloat16)
+        held_ref[step, 0, pair_z, held_rows(half), :] = total
         side_copy(step, 1).start()
-    receivers(1, pair_ref)
-
-    def pass_on(step):
         for k in range(2):
             far_wait(step, k)
             side_copy(step, 2 + k).start()
 
-    pass_on(0)
-
-    def body(step, carry):
+    def take(step):
         for o in range(QUAD):
             side_copy(step, o).wait_recv()
         sources(step)
 
-        @pl.when(step < rounds - 1)
+    xa_ref[:, span:, :] = jnp.zeros((QUAD, xa_ref.shape[1] - span, xa_ref.shape[2]), jnp.bfloat16)
+    receivers(0, own_ref, turn_ref)
+    row = lax.broadcasted_iota(jnp.int32, spun_ref.shape, 0)
+    lane = lax.broadcasted_iota(jnp.int32, spun_ref.shape, 1)
+    place = lane // BLOCK * QUAD + lane % QUAD
+    meant = jnp.zeros_like(lane)
+    for c in range(channels):
+        meant = jnp.where(place == c, pair_line[c], meant)
+    hit = (lane % BLOCK // QUAD * channels + meant) == row
+    spun_ref[...] = jnp.where(hit, 1.0, 0.0).astype(jnp.bfloat16)
+    pass_on(0)
+    pass_on(1)
+
+    def early(step, carry):
+        take(step)
+        products(step, 0)
+        stack_copy(step, 0).start()
+
+        @pl.when(step == 0)
         def _():
-            pass_on(step + 1)
-
-        products(step)
-
-        @pl.when(step < rounds - 1)
-        def _():
-            stack_copy(step).start()
+            pass_on(2)
 
         return carry
 
-    lax.fori_loop(0, rounds, body, 0)
-
-    for step in range(rounds - 1):
-        stack_copy(step).wait_recv()
-    sums = []
-    for which in range(2):
-        total = res_ref[rounds - 1, which]
+    lax.fori_loop(0, 2, early, 0)
+    for place in range(3, channels):
+        near_wait(place)
+    receivers(1, pair_ref, spun_ref)
+
+    def shared(step, carry):
+        products(step, 1)
+        stack_copy(step, 1).start()
+        return carry
+
+    lax.fori_loop(0, 2, shared, 0)
+    pass_on(3)
+
+    def late(step, carry):
+        take(step)
+
+        def each(index, carry):
+            products(step, 1 - index)
+
+            @pl.when(step < rounds - 1)
+            def _():
+                stack_copy(step, 1 - index).start()
+
+            return carry
+
+        lax.fori_loop(0, 2, each, 0)
+        return carry
+
+    lax.fori_loop(2, rounds, late, 0)
+    totals = []
+    for which in (1, 0):
+        total = res_ref[which]
         for step in range(rounds - 1):
-            total = total + land_ref[step, which]
-        if which == 0:
-            sums.append(total)
-        else:
-            half_ref[...] = total
-    end_copy.start()
+            stack_copy(step, which).wait_recv()
+            total = total + land_ref[step, which].astype(jnp.float32)
+        totals.append(total)
+        if which:
+            half_ref[...] = total.astype(jnp.bfloat16)
+            end_copy.start()
     for step in range(rounds):
         for k in range(2):
             far_copy(step, k).wait_send()
         for o in range(QUAD):
             side_copy(step, o).wait_send()
-    pair_copy.wait_send()
+    for place in range(channels):
+        near_copy(place).wait_send()
     for step in range(rounds - 1):
-        stack_copy(step).wait_send()
+        for which in range(2):
+            stack_copy(step, which).wait_send()
     end_copy.wait_recv()
-    total = sums[0] + part_ref[...]
+    both = totals[1] + part_ref[...].astype(jnp.float32)
     groups = (LAGS - 1) // QUAD
     for side in range(2):
-        lanes = slice(side * BLOCK, (side + 1) * BLOCK)
+        total = both[side * LAGS * channels : (side + 1) * LAGS * channels]
         lined = jnp.concatenate(
             [
                 jnp.concatenate(
-                    [total[(QUAD * g + q) * channels : (QUAD * g + q + 1) * channels, lanes] for g in range(groups)], axis=0
+                    [total[(QUAD * g + q) * channels : (QUAD * g + q + 1) * channels] for g in range(groups)], axis=0
                 )
                 for q in range(QUAD)
             ],
@@ -657,7 +754,7 @@
             for p in (high, middle, low)
         ]
         whole = split[0] + split[1] + split[2]
-        last = total[(LAGS - 1) * channels : LAGS * channels, lanes]
+        last = total[(LAGS - 1) * channels : LAGS * channels]
         for zz in range(QUAD):
             for g in range(groups):
                 fin_ref[side * QUAD + zz, :, g * BLOCK : (g + 1) * BLOCK] = whole[
@@ -695,7 +792,7 @@
     pairs = -(-span // (windows * 4))
     rows = (pairs * 4 + 2 * HALO) * windows
     wide = channels * STEP
-    stack = (LAGS * channels, 2 * BLOCK)
+    stack = (2 * LAGS * channels, BLOCK)
     bf16, f32 = jnp.bfloat16, jnp.float32
     dma = pltpu.SemaphoreType.DMA
     return pl.pallas_call(
@@ -705,28 +802,31 @@
         + [pl.BlockSpec(memory_space=pltpu.VMEM)] * len(tables),
         out_specs=pl.BlockSpec(memory_space=pltpu.VMEM),
         scratch_shapes=[
+            pltpu.VMEM((channels, span + HALO * windows, BLOCK), bf16),
             pltpu.VMEM((channels, rows, BLOCK), bf16),
             pltpu.VMEM((channels, rows, BLOCK), bf16),
             pltpu.VMEM((rounds, depth, BLOCK), bf16),
             pltpu.VMEM((rounds, 2, QUAD, rows, BLOCK), bf16),
+            pltpu.VMEM((wide, wide), bf16),
             pltpu.VMEM((QUAD, pairs * 4 * windows, wide), bf16),
             pltpu.VMEM((TONES, 2, pairs * 2 * windows, wide), bf16),
-            pltpu.VMEM((2, TONES, 2, wide, pairs * 4 * windows), bf16),
+            pltpu.VMEM((2, TONES, 2, wide // 2, pairs * 8 * windows), bf16),
             pltpu.VMEM((QUAD, rows, 2 * BLOCK), bf16),
-            pltpu.VMEM((TONES, pairs * 4 * windows, 2 * BLOCK), bf16),
+            pltpu.VMEM((rounds, TONES, pairs * 8 * windows, 2 * BLOCK), bf16),
             pltpu.VMEM((2, TONES * 2 * channels, 2 * BLOCK), f32),
-            pltpu.VMEM((rounds, 2, *stack), f32),
-            pltpu.VMEM((rounds - 1, 2, *stack), f32),
-            pltpu.VMEM(stack, f32),
-            pltpu.VMEM(stack, f32),
+            pltpu.VMEM((2, *stack), f32),
+            pltpu.VMEM((rounds, 2, *stack), bf16),
+            pltpu.VMEM((rounds - 1, 2, *stack), bf16),
+            pltpu.VMEM(stack, bf16),
+            pltpu.VMEM(stack, bf16),
             pltpu.VMEM((per_round, channels, 2 * MAX_LAG + BLOCK), f32),
-            dma((2,)),
+            dma((2, channels)),
             dma((rounds, 2)),
             dma((rounds, 2)),
             dma((rounds, QUAD)),
             dma((rounds, QUAD)),
-            dma((rounds - 1,)),
-            dma((rounds - 1,)),
+            dma((rounds - 1, 2)),
+            dma((rounds - 1, 2)),
             dma((2,)),
         ],
         compiler_params=pltpu.CompilerParams(

time: 83.1 us -> 50.8 us (0.61)
  the two profiles are of different devices: /device:TPU:10 before, /device:TPU:0 now
where the time goes in v2:
time: 50.8 us; the launch traced here: 50.7 us
  Pallas kernels  46.7 us (92%)
  other arithmetic  2.1 us (4%)
  local copies, waits for them, and re-layouts  1.86 us (4%)
    pallas_call x1, Pallas kernels, correlate_halves(): pl.pallas_call(functools.partial(halves_kernel, windows), out_shape=jax.S...  46.7 us
    reduce_sum x1, other arithmetic, whiten(): mean_square = jnp.mean(strain * strain, axis=-1, keepdims=True)  1.91 us
    unnamed x17, local copies, waits for them, and re-layouts  1.8 us

profile of v2, /device:TPU:0, one launch (start us, length us, event | category | flops | bytes accessed | tf_op | source)
XLA Modules:
  0.0 50.7 jit_solution(3720377133870186827)
XLA Ops:
  0.0 0.0 copy-start.7
  0.0 1.9 %multiply_reduce_fusion = f32[8,8]{1,0:T(8,128)S(1)} fusion(f32[8,8,7500]{2,1,0:T(8,128)} %param.8), kind=kLoop, calls=%fused_computation.1 | loop fusion | flops 959936 | bytes 1920256 | tf_op jit(solution)/shard_map/reduce_sum | solution.py:18
  1.9 0.2 copy-done.7
  2.1 0.0 copy-start
  2.1 0.0 copy-start.1
  2.1 0.0 copy-start.2
  2.1 0.0 copy-start.3
  2.1 0.0 copy-start.4
  2.1 0.0 copy-start.5
  2.2 0.0 copy-start.6
  2.2 0.2 multiply_convert_fusion
  2.3 0.1 pad_bitcast_fusion.pieces_ref
  2.4 0.7 %copy-done = bf16[512,512]{1,0:T(8,128)(2,1)S(1)} copy-done((bf16[512,512]{1,0:T(8,128)(2,1)S(1)}, bf16[512,512]{1,0:T(8,128)(2,1)}, u32[]{:S(2)}) %copy-start) | copy-done | bytes 524312
  3.2 0.0 copy-done.1
  3.2 0.0 copy-done.2
  3.2 0.0 copy-done.3
  3.3 0.0 copy-done.4
  3.3 0.0 copy-done.5
  3.3 0.0 copy-done.6
  3.3 46.7 %shard_map.82 = f32[8,8,513]{2,1,0:T(8,128)S(1)} custom-call(bf16[8,480,128]{2,1,0:T(8,128)(2,1)S(1)} %pad_bitcast_fusion.pieces_ref, s32[4,8]{1,0:T(4,128)S(1)} %copy-done.6, bf16[512,512]{1,0:T(8,128)(2,1)S(1)} %copy-done, bf16[256,256]{1,0:T(8,128)(2,1)S(1)} %copy-done.3, bf16[384,128]{1,0:T(8,128)(2,1)S(1)} %copy-done.5, bf16[384,256]{1,0:T(8,128)(2,1)S(1)} %copy-done.1, ...), custom_call_target="tpu_custom_call" | custom-call | tf_op jit(solution)/shard_map/pallas_call | solution.py:798
  50.0 0.7 %copy.10 = f32[8,8,513]{2,1,0:T(8,128)} copy(f32[8,8,513]{2,1,0:T(8,128)S(1)} %shard_map.82) | data formatting | bytes 262656
  (1 shorter events, 0.0 us)
Async XLA Ops:
  0.0 2.1 %copy-start.7 = (f32[8,8,7500]{2,1,0:T(8,128)S(1)}, f32[8,8,7500]{2,1,0:T(8,128)}, u32[]{:S(2)}) copy-start(f32[8,8,7500]{2,1,0:T(8,128)} %param.8) | copy-start | bytes 5760004
  2.1 1.0 %copy-start = (bf16[512,512]{1,0:T(8,128)(2,1)S(1)}, bf16[512,512]{1,0:T(8,128)(2,1)}, u32[]{:S(2)}) copy-start(bf16[512,512]{1,0:T(8,128)(2,1)} %constant.22.clone.perm_ref) | copy-start | bytes 1572868
  2.1 1.1 %copy-start.1 = (bf16[384,256]{1,0:T(8,128)(2,1)S(1)}, bf16[384,256]{1,0:T(8,128)(2,1)}, u32[]{:S(2)}) copy-start(bf16[384,256]{1,0:T(8,128)(2,1)} %constant.25.clone.dft_b_ref) | copy-start | bytes 589828
  2.1 1.1 %copy-start.2 = (f32[136,192]{1,0:T(8,128)S(1)}, f32[136,192]{1,0:T(8,128)}, u32[]{:S(2)}) copy-start(f32[136,192]{1,0:T(8,128)} %constant.27.clone.inverse_ref) | copy-start | bytes 313348
  2.1 1.2 %copy-start.3 = (bf16[256,256]{1,0:T(8,128)(2,1)S(1)}, bf16[256,256]{1,0:T(8,128)(2,1)}, u32[]{:S(2)}) copy-start(bf16[256,256]{1,0:T(8,128)(2,1)} %constant.23.clone.turn_ref) | copy-start | bytes 393220
  2.1 1.2 %copy-start.4 = (f32[12,2,8,128]{3,2,1,0:T(8,128)S(1)}, f32[12,2,8,128]{3,2,1,0:T(8,128)}, u32[]{:S(2)}) copy-start(f32[12,2,8,128]{3,2,1,0:T(8,128)} %constant.26.clone.twist_ref) | copy-start | bytes 294916
  2.1 1.2 %copy-start.5 = (bf16[384,128]{1,0:T(8,128)(2,1)S(1)}, bf16[384,128]{1,0:T(8,128)(2,1)}, u32[]{:S(2)}) copy-start(bf16[384,128]{1,0:T(8,128)(2,1)} %constant.24.clone.dft_a_ref) | copy-start | bytes 294916
  2.2 1.2 %copy-start.6 = (s32[4,8]{1,0:T(4,128)S(1)}, s32[4,8]{1,0:T(4,128)}, u32[]{:S(2)}) copy-start(s32[4,8]{1,0:T(4,128)} %sources_ref.1) | copy-start | bytes 388

commit v3 on v2

--- a/solution.py
+++ b/solution.py
@@ -690,37 +690,44 @@
     def shared(step, carry):
         products(step, 1)
         stack_copy(step, 1).start()
+
+        @pl.when(step == 0)
+        def _():
+            pass_on(3)
+
         return carry
 
     lax.fori_loop(0, 2, shared, 0)
-    pass_on(3)
-
-    def late(step, carry):
-        take(step)
-
-        def each(index, carry):
-            products(step, 1 - index)
-
-            @pl.when(step < rounds - 1)
-            def _():
-                stack_copy(step, 1 - index).start()
-
-            return carry
-
-        lax.fori_loop(0, 2, each, 0)
-        return carry
-
-    lax.fori_loop(2, rounds, late, 0)
-    totals = []
-    for which in (1, 0):
+
+    def summed(which):
         total = res_ref[which]
         for step in range(rounds - 1):
             stack_copy(step, which).wait_recv()
             total = total + land_ref[step, which].astype(jnp.float32)
-        totals.append(total)
-        if which:
-            half_ref[...] = total.astype(jnp.bfloat16)
-            end_copy.start()
+        return total
+
+    def late(step, carry):
+        take(step)
+
+        def each(index, carry):
+            products(step, 1 - index)
+
+            @pl.when(step < rounds - 1)
+            def _():
+                stack_copy(step, 1 - index).start()
+
+            @pl.when((step == rounds - 1) & (index == 0))
+            def _():
+                half_ref[...] = summed(1).astype(jnp.bfloat16)
+                end_copy.start()
+
+            return carry
+
+        lax.fori_loop(0, 2, each, 0)
+        return carry
+
+    lax.fori_loop(2, rounds, late, 0)
+    whole_sum = summed(0)
     for step in range(rounds):
         for k in range(2):
             far_copy(step, k).wait_send()
@@ -732,7 +739,7 @@
         for which in range(2):
             stack_copy(step, which).wait_send()
     end_copy.wait_recv()
-    both = totals[1] + part_ref[...].astype(jnp.float32)
+    both = whole_sum + part_ref[...].astype(jnp.float32)
     groups = (LAGS - 1) // QUAD
     for side in range(2):
         total = both[side * LAGS * channels : (side + 1) * LAGS * channels]

time: 50.8 us -> 48.3 us (0.951)
  Pallas kernels: 46.7 us -> 44.1 us
    pallas_call x1, Pallas kernels: 46.7 us -> 44.1 us  [correlate_halves(): pl.pallas_call(functools.partial(halves_kernel, windows), out_shape=jax.S...]
where the time goes in v3:
time: 48.3 us; the launch traced here: 48.2 us
  Pallas kernels  44.1 us (91%)
  other arithmetic  2.1 us (4%)
  local copies, waits for them, and re-layouts  1.86 us (4%)
    pallas_call x1, Pallas kernels, correlate_halves(): pl.pallas_call(functools.partial(halves_kernel, windows), out_shape=jax.S...  44.1 us
    reduce_sum x1, other arithmetic, whiten(): mean_square = jnp.mean(strain * strain, axis=-1, keepdims=True)  1.91 us
    unnamed x17, local copies, waits for them, and re-layouts  1.8 us

profile of v3, /device:TPU:0, one launch (start us, length us, event | category | flops | bytes accessed | tf_op | source)
XLA Modules:
  0.0 48.2 jit_solution(4887331446173907326)
XLA Ops:
  0.0 0.0 copy-start.7
  0.0 1.9 %multiply_reduce_fusion = f32[8,8]{1,0:T(8,128)S(1)} fusion(f32[8,8,7500]{2,1,0:T(8,128)} %param.8), kind=kLoop, calls=%fused_computation.1 | loop fusion | flops 959936 | bytes 1920256 | tf_op jit(solution)/shard_map/reduce_sum | solution.py:18
  1.9 0.2 copy-done.7
  2.1 0.0 copy-start
  2.1 0.0 copy-start.1
  2.1 0.0 copy-start.2
  2.1 0.0 copy-start.3
  2.1 0.0 copy-start.4
  2.1 0.0 copy-start.5
  2.2 0.0 copy-start.6
  2.2 0.2 multiply_convert_fusion
  2.3 0.1 pad_bitcast_fusion.pieces_ref
  2.4 0.7 %copy-done = bf16[512,512]{1,0:T(8,128)(2,1)S(1)} copy-done((bf16[512,512]{1,0:T(8,128)(2,1)S(1)}, bf16[512,512]{1,0:T(8,128)(2,1)}, u32[]{:S(2)}) %copy-start) | copy-done | bytes 524312
  3.2 0.0 copy-done.1
  3.2 0.0 copy-done.2
  3.2 0.0 copy-done.3
  3.3 0.0 copy-done.4
  3.3 0.0 copy-done.5
  3.3 0.0 copy-done.6
  3.3 44.1 %shard_map.82 = f32[8,8,513]{2,1,0:T(8,128)S(1)} custom-call(bf16[8,480,128]{2,1,0:T(8,128)(2,1)S(1)} %pad_bitcast_fusion.pieces_ref, s32[4,8]{1,0:T(4,128)S(1)} %copy-done.6, bf16[512,512]{1,0:T(8,128)(2,1)S(1)} %copy-done, bf16[256,256]{1,0:T(8,128)(2,1)S(1)} %copy-done.3, bf16[384,128]{1,0:T(8,128)(2,1)S(1)} %copy-done.5, bf16[384,256]{1,0:T(8,128)(2,1)S(1)} %copy-done.1, ...), custom_call_target="tpu_custom_call" | custom-call | tf_op jit(solution)/shard_map/pallas_call | solution.py:805
  47.5 0.7 %copy.10 = f32[8,8,513]{2,1,0:T(8,128)} copy(f32[8,8,513]{2,1,0:T(8,128)S(1)} %shard_map.82) | data formatting | bytes 262656
  (1 shorter events, 0.0 us)
Async XLA Ops:
  0.0 2.1 %copy-start.7 = (f32[8,8,7500]{2,1,0:T(8,128)S(1)}, f32[8,8,7500]{2,1,0:T(8,128)}, u32[]{:S(2)}) copy-start(f32[8,8,7500]{2,1,0:T(8,128)} %param.8) | copy-start | bytes 5760004
  2.1 1.0 %copy-start = (bf16[512,512]{1,0:T(8,128)(2,1)S(1)}, bf16[512,512]{1,0:T(8,128)(2,1)}, u32[]{:S(2)}) copy-start(bf16[512,512]{1,0:T(8,128)(2,1)} %constant.22.clone.perm_ref) | copy-start | bytes 1572868
  2.1 1.1 %copy-start.1 = (bf16[384,256]{1,0:T(8,128)(2,1)S(1)}, bf16[384,256]{1,0:T(8,128)(2,1)}, u32[]{:S(2)}) copy-start(bf16[384,256]{1,0:T(8,128)(2,1)} %constant.25.clone.dft_b_ref) | copy-start | bytes 589828
  2.1 1.1 %copy-start.2 = (f32[136,192]{1,0:T(8,128)S(1)}, f32[136,192]{1,0:T(8,128)}, u32[]{:S(2)}) copy-start(f32[136,192]{1,0:T(8,128)} %constant.27.clone.inverse_ref) | copy-start | bytes 313348
  2.1 1.2 %copy-start.3 = (bf16[256,256]{1,0:T(8,128)(2,1)S(1)}, bf16[256,256]{1,0:T(8,128)(2,1)}, u32[]{:S(2)}) copy-start(bf16[256,256]{1,0:T(8,128)(2,1)} %constant.23.clone.turn_ref) | copy-start | bytes 393220
  2.1 1.2 %copy-start.4 = (f32[12,2,8,128]{3,2,1,0:T(8,128)S(1)}, f32[12,2,8,128]{3,2,1,0:T(8,128)}, u32[]{:S(2)}) copy-start(f32[12,2,8,128]{3,2,1,0:T(8,128)} %constant.26.clone.twist_ref) | copy-start | bytes 294916
  2.1 1.2 %copy-start.5 = (bf16[384,128]{1,0:T(8,128)(2,1)S(1)}, bf16[384,128]{1,0:T(8,128)(2,1)}, u32[]{:S(2)}) copy-start(bf16[384,128]{1,0:T(8,128)(2,1)} %constant.24.clone.dft_a_ref) | copy-start | bytes 294916
  2.2 1.2 %copy-start.6 = (s32[4,8]{1,0:T(4,128)S(1)}, s32[4,8]{1,0:T(4,128)}, u32[]{:S(2)}) copy-start(s32[4,8]{1,0:T(4,128)} %sources_ref.1) | copy-start | bytes 388

commit v4 on v3

--- a/solution.py
+++ b/solution.py
@@ -333,13 +333,15 @@
     angle = np.outer(np.arange(LAGS), tones())
     back = np.stack([np.cos(angle), -np.sin(angle)], axis=2) * (factor / TONES / scales**2)[:, None]
     inverse = np.einsum("kfv,cd->kcfvd", back, np.eye(channels)).reshape(LAGS * channels, TONES * 2 * channels)
+    inverse = np.pad(inverse, ((0, -inverse.shape[0] % 16), (0, 0)))
+    upper = inverse.astype(bf16)
     return (
         jnp.asarray(perm.astype(bf16)),
         jnp.asarray(turn.astype(bf16)),
         jnp.asarray(dft(TAPS).astype(bf16)),
         jnp.asarray(dft(POINTS).astype(bf16)),
         jnp.asarray(np.ascontiguousarray(twist).astype(np.float32)),
-        jnp.asarray(inverse.astype(np.float32)),
+        jnp.asarray(np.concatenate([upper, (inverse - upper.astype(np.float64)).astype(bf16)], axis=0)),
     )
 
 
@@ -628,9 +630,13 @@
             return carry
 
         lax.fori_loop(0, TONES, tone, 0, unroll=12)
-        sums = jnp.dot(
-            inverse_ref[...], spec_ref[which], precision=lax.Precision.HIGHEST, preferred_element_type=jnp.float32
-        )
+        rows = inverse_ref.shape[0] // 2
+        seen = spec_ref[which]
+        high = seen.astype(jnp.bfloat16)
+        low = (seen - high.astype(jnp.float32)).astype(jnp.bfloat16)
+        sums = jnp.dot(inverse_ref[...], high, preferred_element_type=jnp.float32)
+        sums = sums[:rows] + sums[rows:] + jnp.dot(inverse_ref[:rows], low, preferred_element_type=jnp.float32)
+        sums = sums[: LAGS * channels]
         sums = jnp.concatenate([sums[:, :BLOCK], sums[:, BLOCK:]], axis=0)
         res_ref[which] = sums
         sent_ref[step, which] = sums.astype(jnp.bfloat16)

time: 48.3 us -> 48.1 us (level)
  no operation moved by 1% of the time
where the time goes in v4:
time: 48.1 us; the launch traced here: 47.9 us
  Pallas kernels  43.9 us (91%)
  other arithmetic  2.1 us (4%)
  local copies, waits for them, and re-layouts  1.87 us (4%)
    pallas_call x1, Pallas kernels, correlate_halves(): pl.pallas_call(functools.partial(halves_kernel, windows), out_shape=jax.S...  43.9 us
    reduce_sum x1, other arithmetic, whiten(): mean_square = jnp.mean(strain * strain, axis=-1, keepdims=True)  1.91 us
    unnamed x17, local copies, waits for them, and re-layouts  1.8 us

profile of v4, /device:TPU:0, one launch (start us, length us, event | category | flops | bytes accessed | tf_op | source)
XLA Modules:
  0.0 47.9 jit_solution(3774730145838744522)
XLA Ops:
  0.0 0.0 copy-start.7
  0.0 1.9 %multiply_reduce_fusion = f32[8,8]{1,0:T(8,128)S(1)} fusion(f32[8,8,7500]{2,1,0:T(8,128)} %param.8), kind=kLoop, calls=%fused_computation.1 | loop fusion | flops 959936 | bytes 1920256 | tf_op jit(solution)/shard_map/reduce_sum | solution.py:18
  1.9 0.2 copy-done.7
  2.1 0.0 copy-start
  2.1 0.0 copy-start.1
  2.1 0.0 copy-start.2
  2.1 0.0 copy-start.3
  2.1 0.0 copy-start.4
  2.1 0.0 copy-start.5
  2.2 0.0 copy-start.6
  2.2 0.2 multiply_convert_fusion
  2.3 0.1 pad_bitcast_fusion.pieces_ref
  2.4 0.7 %copy-done = bf16[512,512]{1,0:T(8,128)(2,1)S(1)} copy-done((bf16[512,512]{1,0:T(8,128)(2,1)S(1)}, bf16[512,512]{1,0:T(8,128)(2,1)}, u32[]{:S(2)}) %copy-start) | copy-done | bytes 524312
  3.2 0.0 copy-done.1
  3.2 0.0 copy-done.2
  3.2 0.0 copy-done.3
  3.3 0.0 copy-done.4
  3.3 0.0 copy-done.5
  3.3 0.0 copy-done.6
  3.3 43.9 %shard_map.82 = f32[8,8,513]{2,1,0:T(8,128)S(1)} custom-call(bf16[8,480,128]{2,1,0:T(8,128)(2,1)S(1)} %pad_bitcast_fusion.pieces_ref, s32[4,8]{1,0:T(4,128)S(1)} %copy-done.6, bf16[512,512]{1,0:T(8,128)(2,1)S(1)} %copy-done, bf16[256,256]{1,0:T(8,128)(2,1)S(1)} %copy-done.3, bf16[384,128]{1,0:T(8,128)(2,1)S(1)} %copy-done.5, bf16[384,256]{1,0:T(8,128)(2,1)S(1)} %copy-done.1, ...), custom_call_target="tpu_custom_call" | custom-call | tf_op jit(solution)/shard_map/pallas_call | solution.py:811
  47.3 0.7 %copy.10 = f32[8,8,513]{2,1,0:T(8,128)} copy(f32[8,8,513]{2,1,0:T(8,128)S(1)} %shard_map.82) | data formatting | bytes 262656
  (1 shorter events, 0.0 us)
Async XLA Ops:
  0.0 2.1 %copy-start.7 = (f32[8,8,7500]{2,1,0:T(8,128)S(1)}, f32[8,8,7500]{2,1,0:T(8,128)}, u32[]{:S(2)}) copy-start(f32[8,8,7500]{2,1,0:T(8,128)} %param.8) | copy-start | bytes 5760004
  2.1 1.0 %copy-start = (bf16[512,512]{1,0:T(8,128)(2,1)S(1)}, bf16[512,512]{1,0:T(8,128)(2,1)}, u32[]{:S(2)}) copy-start(bf16[512,512]{1,0:T(8,128)(2,1)} %constant.22.clone.perm_ref) | copy-start | bytes 1572868
  2.1 1.1 %copy-start.1 = (bf16[384,256]{1,0:T(8,128)(2,1)S(1)}, bf16[384,256]{1,0:T(8,128)(2,1)}, u32[]{:S(2)}) copy-start(bf16[384,256]{1,0:T(8,128)(2,1)} %constant.25.clone.dft_b_ref) | copy-start | bytes 589828
  2.1 1.1 %copy-start.2 = (bf16[288,192]{1,0:T(8,128)(2,1)S(1)}, bf16[288,192]{1,0:T(8,128)(2,1)}, u32[]{:S(2)}) copy-start(bf16[288,192]{1,0:T(8,128)(2,1)} %constant.27.clone.inverse_ref) | copy-start | bytes 331780
  2.1 1.2 %copy-start.3 = (bf16[256,256]{1,0:T(8,128)(2,1)S(1)}, bf16[256,256]{1,0:T(8,128)(2,1)}, u32[]{:S(2)}) copy-start(bf16[256,256]{1,0:T(8,128)(2,1)} %constant.23.clone.turn_ref) | copy-start | bytes 393220
  2.1 1.2 %copy-start.4 = (f32[12,2,8,128]{3,2,1,0:T(8,128)S(1)}, f32[12,2,8,128]{3,2,1,0:T(8,128)}, u32[]{:S(2)}) copy-start(f32[12,2,8,128]{3,2,1,0:T(8,128)} %constant.26.clone.twist_ref) | copy-start | bytes 294916
  2.1 1.2 %copy-start.5 = (bf16[384,128]{1,0:T(8,128)(2,1)S(1)}, bf16[384,128]{1,0:T(8,128)(2,1)}, u32[]{:S(2)}) copy-start(bf16[384,128]{1,0:T(8,128)(2,1)} %constant.24.clone.dft_a_ref) | copy-start | bytes 294916
  2.2 1.2 %copy-start.6 = (s32[4,8]{1,0:T(4,128)S(1)}, s32[4,8]{1,0:T(4,128)}, u32[]{:S(2)}) copy-start(s32[4,8]{1,0:T(4,128)} %sources_ref.1) | copy-start | bytes 388
